TPU v7x, 32 devices: a whole 2x2x4 slice. The times are simulated.
32 devices in a mesh: cohort: 2 (over y), people: 4 (over z), markers: 4 (over x, core).
Axes of the slice: x: 2, y: 2, z: 4, core: 2. Of those that a mesh axis runs over, the one named last changes fastest.
Arguments:
- genotype: int32 [12288, 2048], P(('cohort', 'people'), 'markers'), parts along dimension 0, may hold values from 0 to 170, as said below
- allele_freq: float32 [16384], P(('cohort', 'markers')), parts along dimension 0, may hold values from 0.05 to 0.5
- person_weight: float32 [12288], P(('cohort', 'people')), parts along dimension 0, may hold values from 0.5 to 18, as said below
- basis: bfloat16 [64, 8192], P('cohort', 'markers'), parts along dimension 0, may hold values from -0.0625 to 0.0625
- residuals: bfloat16 [128, 6144], P('cohort', 'people'), parts along dimension 0, may hold values from -6 to 6
- block_markers: int32 [2048], P('markers'), may hold values from 0 to 8191, as said below
Outputs:
- components: float32 [64, 6144], P('cohort', 'people'), parts along dimension 0
- coefficients: float32 [64, 64], P('cohort'), parts along dimension 0
- basis_next: float32 [4, 64, 2048], P('markers', 'cohort', 'people'), parts along dimension 1
- scores: float32 [4, 128, 512], P('markers', 'cohort', 'people'), parts along dimension 1
There are 2 independent parts, one for each index of `cohort`. A program takes and returns all parts, laid end to end along the dimension named above; an argument that names none is the same for every part. Nothing has to cross between parts.
Inputs may be any that keep to these rules, and one draw needn't show every extreme that they name: `genotype`: each word packs the dosages (0, 1 or 2) of four consecutive markers of one person, marker 4 w + j in bits 2 j and 2 j + 1. `block_markers`: the j-th run of 512 entries holds distinct increasing markers among j * 2048 to (j + 1) * 2048 - 1, always including both of these ends. `person_weight`: positive weights.
All inputs are finite; a program needn't handle non-finite values.
Results may differ from a plain program's by a relative error of at most 0.0054.
Values sent between devices are 32-bit elements; how exact they have to be, the bound alone decides.
A program may use at most 128 MiB of HBM per device.

v0:
```python
import functools
import math

import jax
import jax.numpy as jnp
from jax import lax
from jax.experimental import pallas as pl
from jax.experimental.pallas import tpu as pltpu
from jax.sharding import PartitionSpec as P

MESH = pl.DeviceIdType.MESH


def from_partner(block, axis, apart):
    count = lax.axis_size(axis)
    route = []
    for low in range(count):
        high = low | 1 << apart
        if high != low and high < count:
            route += [(low, high), (high, low)]
    return lax.ppermute(block, axis, route)


def decode(packed, freq, weight):
    shifts = 2 * jnp.arange(4, dtype=jnp.int32)
    dosage = jnp.bitwise_and(jnp.right_shift(packed[:, :, None], shifts[None, None, :]), 3)
    dosage = dosage.reshape(packed.shape[0], packed.shape[1] * 4).astype(jnp.float32)
    standard = (dosage - 2.0 * freq[None, :]) / jnp.sqrt(2.0 * freq * (1.0 - freq))[None, :]
    return (weight[:, None] * standard).astype(jnp.bfloat16)


def shards(genotype, allele_freq, person_weight, basis, residuals, block_markers):
    weighted = decode(genotype, allele_freq, person_weight)
    rows_here = weighted.shape[0]
    marker_cols = weighted.shape[1]
    marker_count = lax.axis_size("markers")
    marker_index = lax.axis_index("markers")
    share_rows = rows_here // marker_count
    partial_value = lax.dot_general(
        basis, weighted, (((1,), (1,)), ((), ())), preferred_element_type=jnp.float32
    )
    full_sketch = lax.psum(partial_value, "markers")
    own_sketch = lax.dynamic_slice_in_dim(full_sketch, marker_index * share_rows, share_rows, 1)
    own_residual = lax.dynamic_slice_in_dim(
        residuals, marker_index * share_rows, share_rows, 1
    ).astype(jnp.float32)
    gram_local = jnp.dot(own_sketch, own_sketch.T, precision=lax.Precision.HIGHEST)
    factor_up = jnp.linalg.cholesky(gram_local).T
    levels = lax.axis_size(("people", "markers")).bit_length() - 1
    for level in range(levels):
        partner = from_partner(factor_up, ("people", "markers"), level)
        combined = jnp.dot(factor_up.T, factor_up, precision=lax.Precision.HIGHEST) + jnp.dot(
            partner.T, partner, precision=lax.Precision.HIGHEST
        )
        factor_up = jnp.linalg.cholesky(combined).T
    factor_low = factor_up.T
    ortho = jax.scipy.linalg.solve_triangular(factor_low, full_sketch, lower=True)
    ortho_share = lax.dynamic_slice_in_dim(ortho, marker_index * share_rows, share_rows, 1)
    coefficients = lax.psum(
        jnp.dot(ortho_share, own_residual.T, precision=lax.Precision.HIGHEST), ("people", "markers")
    )
    projected = (
        residuals.astype(jnp.float32)
        - jnp.dot(coefficients.T, ortho, precision=lax.Precision.HIGHEST)
    ).astype(jnp.bfloat16)
    ortho_half = ortho.astype(jnp.bfloat16)
    basis_partial = jnp.dot(ortho_half, weighted, preferred_element_type=jnp.float32)
    columns = block_markers - marker_index * marker_cols
    chosen = jnp.take(weighted, columns, axis=1)
    score_partial = jnp.dot(projected, chosen, preferred_element_type=jnp.float32)
    people_count = lax.axis_size("people")
    people_index = lax.axis_index("people")
    basis_total, score_total = lax.psum((basis_partial, score_partial), "people")
    basis_width = basis_total.shape[1] // people_count
    score_width = score_total.shape[1] // people_count
    basis_own = lax.dynamic_slice_in_dim(basis_total, people_index * basis_width, basis_width, 1)
    score_own = lax.dynamic_slice_in_dim(score_total, people_index * score_width, score_width, 1)
    total_people = rows_here * people_count
    root_people = math.sqrt(total_people)
    components = root_people * ortho
    scores = (score_own / root_people)[None]
    return (components, coefficients, basis_own[None], scores)


ROWS_STEP = 128
TILE = 128


def split3(value):
    first = value.astype(jnp.bfloat16)
    left = value - first.astype(jnp.float32)
    second = left.astype(jnp.bfloat16)
    third = (left - second.astype(jnp.float32)).astype(jnp.bfloat16)
    return jnp.concatenate([first, second, third], axis=0)


def sum3(value):
    third = value.shape[0] // 3
    return value[:third] + value[third : 2 * third] + value[2 * third :]


def mm(left, right):
    return jnp.dot(left, right, preferred_element_type=jnp.float32)


def mm_nt(left, right, precision=None):
    return lax.dot_general(
        left,
        right,
        (((1,), (1,)), ((), ())),
        preferred_element_type=jnp.float32,
        precision=precision,
    )


def eliminate(full, count):
    rows = lax.broadcasted_iota(jnp.int32, full.shape, 0)
    lanes = lax.broadcasted_iota(jnp.int32, full.shape, 1)
    for k in range(count):
        column = jnp.broadcast_to(full[:, k : k + 1], full.shape)
        row = full[k : k + 1, :] * (1.0 / column[k : k + 1, :])
        full = jnp.where(rows > k, full - column * row, full)
    pivots = jnp.sum(jnp.where(rows == lanes, full, 0.0), axis=1, keepdims=True)
    return full * (1.0 / jnp.sqrt(pivots))


def kernel(
    root_people,
    geno_hbm,
    freq_hbm,
    weight_hbm,
    basis_hbm,
    resid_hbm,
    block_hbm,
    comp_hbm,
    coef_hbm,
    next_hbm,
    score_hbm,
    comp_ref,
    coef_ref,
    next_ref,
    score_ref,
    geno,
    freq_ref,
    weight_ref,
    basis_ref,
    resid_ref,
    block_ref,
    wt,
    hot,
    perm,
    freq_rows,
    basis_rows,
    part,
    part_in,
    sketch_all,
    resid_score,
    resid_score_in,
    gram_all,
    next_part,
    next_in,
    chosen_part,
    chosen_in,
    geno_sem,
    load_sem,
    store_sem,
    send_sem,
    recv_sem,
):
    people = lax.axis_index("people")
    markers = lax.axis_index("markers")
    n = 4
    k_count, share = part.shape[1], part.shape[2]
    block = wt.shape[2]
    words = block // 4
    marker_peer = [lax.rem(markers + d, n) for d in range(n)]
    people_peer = [lax.rem(people + d, n) for d in range(n)]
    order = [1, 2, 3, 0]

    small = []
    for i, (src, dst) in enumerate(
        (
            (freq_hbm, freq_ref),
            (basis_hbm, basis_ref),
            (weight_hbm, weight_ref),
            (block_hbm, block_ref),
            (resid_hbm, resid_ref),
        )
    ):
        small.append(pltpu.make_async_copy(src, dst, load_sem.at[i]))
        small[-1].start()
    for step, d in enumerate(order):
        at = pl.ds(pl.multiple_of(marker_peer[d] * share, share), share)
        pltpu.make_async_copy(geno_hbm.at[at], geno.at[at], geno_sem.at[step]).start()

    barrier = pltpu.get_barrier_semaphore()
    for d in range(1, n):
        pl.semaphore_signal(
            barrier, inc=1, device_id={"markers": marker_peer[d]}, device_id_type=MESH
        )
        pl.semaphore_signal(
            barrier, inc=1, device_id={"people": people_peer[d]}, device_id_type=MESH
        )

    sends = {}

    def send(group, d, src, dst, axis):
        peer = marker_peer[d] if axis == "markers" else people_peer[d]
        copy = pltpu.make_async_remote_copy(
            src_ref=src,
            dst_ref=dst,
            send_sem=send_sem.at[group, d - 1],
            recv_sem=recv_sem.at[group, d - 1],
            device_id={axis: peer},
            device_id_type=MESH,
        )
        copy.start()
        sends[group, d] = copy

    marker = lax.broadcasted_iota(jnp.int32, (block, block), 0)
    place = lax.broadcasted_iota(jnp.int32, (block, block), 1)
    perm[...] = jnp.where(
        marker == 4 * lax.rem(place, words) + lax.div(place, words), 1.0, 0.0
    ).astype(jnp.bfloat16)
    small[0].wait()
    small[1].wait()
    small[2].wait()
    freq = jnp.concatenate([freq_ref[:, c * block : (c + 1) * block] for c in range(n)], axis=0)
    freq = jnp.concatenate([freq, freq], axis=0)
    freq = sum3(mm(split3(freq), perm[...]))[:n]
    freq_rows[0:n, :] = 2.0 * freq
    freq_rows[n : 2 * n, :] = 1.0 / jnp.sqrt(2.0 * freq * (1.0 - freq))
    basis = jnp.concatenate([basis_ref[:, c * block : (c + 1) * block] for c in range(n)], axis=0)
    basis_rows[...] = mm(basis, perm[...]).astype(jnp.bfloat16)

    pl.semaphore_wait(barrier, 2 * (n - 1))

    def share_copy(slot, target):
        return pltpu.make_async_remote_copy(
            src_ref=part.at[target],
            dst_ref=part_in.at[slot],
            send_sem=send_sem.at[0, slot],
            recv_sem=recv_sem.at[0, slot],
            device_id={"markers": target},
            device_id_type=MESH,
        )

    def decode(step, carry):
        target = lax.rem(markers + step + 1, n)
        at = pl.ds(pl.multiple_of(target * share, share), share)
        pltpu.make_async_copy(geno_hbm.at[at], geno.at[at], geno_sem.at[step]).wait()
        weight = []
        for i in range(share // ROWS_STEP):
            line = weight_ref[pl.ds(target * (share // ROWS_STEP) + i, 1), :]
            weight.append(jnp.transpose(jnp.broadcast_to(line, (ROWS_STEP, TILE))))
        weight = jnp.concatenate(weight, axis=0)
        total = None
        for c in range(n):
            packed = geno[at, c * words : (c + 1) * words]
            tiles = []
            for j in range(4):
                cols = slice(j * words, (j + 1) * words)
                dosage = jnp.bitwise_and(jnp.right_shift(packed, 2 * j), 3).astype(jnp.float32)
                value = (dosage - freq_rows[c : c + 1, cols]) * freq_rows[n + c : n + c + 1, cols]
                tiles.append((weight * value).astype(jnp.bfloat16))
            tile = jnp.concatenate(tiles, axis=1)
            wt[c, at, :] = tile
            got = mm_nt(basis_rows[c * k_count : (c + 1) * k_count, :], tile)
            total = got if total is None else total + got
        part[target] = total

        @pl.when(step < n - 1)
        def _():
            share_copy(step, target).start()

        return carry

    lax.fori_loop(0, n, decode, 0)
    for d in range(1, n):
        sends[0, d] = share_copy(d - 1, marker_peer[d])

    small[3].wait()
    small[4].wait()
    local = block_ref[...] - markers * (n * block)
    inner = lax.rem(local, block)
    column = lax.div(local, block) * block + lax.rem(inner, 4) * words + lax.div(inner, 4)
    for c in range(n):
        row = lax.broadcasted_iota(jnp.int32, (block, hot.shape[2]), 0) + c * block
        hot[c] = jnp.where(row == column, 1.0, 0.0).astype(jnp.bfloat16)

    for d in range(1, n):
        sends[0, d].wait_recv()
    sketch_all[markers] = part[markers] + part_in[0] + part_in[1] + part_in[2]
    for d in range(1, n):
        send(1, d, sketch_all.at[markers], sketch_all.at[markers], "markers")

    resid = resid_ref[...]
    picked = None
    for c in range(n):
        got = mm(split3(mm(resid, wt[c])), hot[c])
        picked = got if picked is None else picked + got
    picked = sum3(picked)
    width = picked.shape[1] // n
    for c in range(n):
        resid_score[c] = picked[:, c * width : (c + 1) * width]
    for d in range(1, n):
        send(2, d, resid_score.at[people_peer[d]], resid_score_in.at[d - 1], "people")

    for d in range(1, n):
        sends[1, d].wait_recv()
    sketch = jnp.concatenate([sketch_all[c] for c in range(n)], axis=1)
    both = jnp.concatenate([sketch, resid.astype(jnp.float32)], axis=0)
    gram = mm_nt(sketch, both, lax.Precision.HIGHEST)
    pad = jnp.zeros((k_count, TILE - gram.shape[1]), jnp.float32)
    gram_all[people] = jnp.concatenate([gram, pad], axis=1)
    for d in range(1, n):
        send(3, d, gram_all.at[people], gram_all.at[people], "people")

    pieces = split3(sketch)
    picked = None
    for d in (2, 1, 3, 0):
        c = people_peer[d]
        total = sum3(mm(pieces, wt[c]))
        next_part[c] = total
        if d:
            send(4, d, next_part.at[c], next_in.at[d - 1], "people")
        got = mm(split3(total), hot[c])
        picked = got if picked is None else picked + got
    picked = sum3(picked)
    for c in range(n):
        chosen_part[c] = picked[:, c * width : (c + 1) * width]
    for d in range(1, n):
        send(5, d, chosen_part.at[people_peer[d]], chosen_in.at[d - 1], "people")

    for d in range(1, n):
        sends[3, d].wait_recv()
    full = gram_all[0] + gram_all[1] + gram_all[2] + gram_all[3]
    lane = lax.broadcasted_iota(jnp.int32, full.shape, 1)
    line = lax.broadcasted_iota(jnp.int32, full.shape, 0)
    full = jnp.where(lane == line + (TILE - k_count), 1.0, full)
    full = eliminate(full, k_count)
    coef = full[:, k_count : TILE - k_count]
    inverse = full[:, TILE - k_count :]
    coef_ref[...] = coef
    comp_ref[...] = root_people * jnp.dot(
        inverse, sketch, preferred_element_type=jnp.float32, precision=lax.Precision.HIGHEST
    )
    stores = [
        pltpu.make_async_copy(src, dst, store_sem.at[i])
        for i, (src, dst) in enumerate(
            (
                (coef_ref, coef_hbm),
                (comp_ref, comp_hbm),
                (next_ref, next_hbm),
                (score_ref, score_hbm),
            )
        )
    ]
    stores[0].start()
    stores[1].start()

    for d in range(1, n):
        sends[2, d].wait_recv()
        sends[4, d].wait_recv()
        sends[5, d].wait_recv()
    total = next_part[people] + next_in[0] + next_in[1] + next_in[2]
    chosen = chosen_part[people] + chosen_in[0] + chosen_in[1] + chosen_in[2]
    scored = resid_score[people] + resid_score_in[0] + resid_score_in[1] + resid_score_in[2]
    solved = jnp.dot(
        inverse,
        jnp.concatenate([total, chosen], axis=1),
        preferred_element_type=jnp.float32,
        precision=lax.Precision.HIGHEST,
    )
    next_ref[0] = sum3(mm_nt(split3(solved[:, :block]), perm[...]))
    stores[2].start()
    removed = lax.dot_general(
        coef,
        solved[:, block:],
        (((0,), (0,)), ((), ())),
        preferred_element_type=jnp.float32,
        precision=lax.Precision.HIGHEST,
    )
    score_ref[0] = (scored - removed) * (1.0 / root_people)
    stores[3].start()
    for store in stores:
        store.wait()
    for copy in sends.values():
        copy.wait_send()


def write_results(*refs):
    sources, results, held, (load_sem, store_sem) = refs[:4], refs[4:8], refs[8:12], refs[12:]
    loads = [pltpu.make_async_copy(sources[i], held[i], load_sem.at[i]) for i in range(4)]
    stores = [pltpu.make_async_copy(held[i], results[i], store_sem.at[i]) for i in range(4)]
    for load in loads:
        load.start()
    for load, store in zip(loads, stores):
        load.wait()
        store.start()
    for store in stores:
        store.wait()


def fused(genotype, allele_freq, person_weight, basis, residuals, block_markers):
    n = 4
    rows, words = genotype.shape
    k_count = basis.shape[0]
    r_count = residuals.shape[0]
    share = rows // n
    block = 4 * words // n
    picks = block_markers.shape[0]
    width = picks // n
    f32, bf16 = jnp.float32, jnp.bfloat16
    hbm = pl.BlockSpec(memory_space=pltpu.HBM)
    root_people = math.sqrt(rows * n)
    shapes = (
        jax.ShapeDtypeStruct((k_count, rows), f32),
        jax.ShapeDtypeStruct((k_count, r_count), f32),
        jax.ShapeDtypeStruct((1, k_count, block), f32),
        jax.ShapeDtypeStruct((1, r_count, width), f32),
    )
    results = pl.pallas_call(
        functools.partial(kernel, root_people),
        out_shape=shapes,
        in_specs=[hbm] * 6,
        out_specs=(hbm,) * 4,
        scratch_shapes=[
            pltpu.VMEM((k_count, rows), f32),
            pltpu.VMEM((k_count, r_count), f32),
            pltpu.VMEM((1, k_count, block), f32),
            pltpu.VMEM((1, r_count, width), f32),
            pltpu.VMEM((rows, words), jnp.int32),
            pltpu.VMEM((1, n * block), f32),
            pltpu.VMEM((rows // TILE, TILE), f32),
            pltpu.VMEM(basis.shape, bf16),
            pltpu.VMEM(residuals.shape, bf16),
            pltpu.VMEM((1, picks), jnp.int32),
            pltpu.VMEM((n, rows, block), bf16),
            pltpu.VMEM((n, block, picks), bf16),
            pltpu.VMEM((block, block), bf16),
            pltpu.VMEM((2 * n, block), f32),
            pltpu.VMEM((n * k_count, block), bf16),
            pltpu.VMEM((n, k_count, share), f32),
            pltpu.VMEM((n - 1, k_count, share), f32),
            pltpu.VMEM((n, k_count, share), f32),
            pltpu.VMEM((n, r_count, width), f32),
            pltpu.VMEM((n - 1, r_count, width), f32),
            pltpu.VMEM((n, k_count, TILE), f32),
            pltpu.VMEM((n, k_count, block), f32),
            pltpu.VMEM((n - 1, k_count, block), f32),
            pltpu.VMEM((n, k_count, width), f32),
            pltpu.VMEM((n - 1, k_count, width), f32),
            pltpu.SemaphoreType.DMA((n,)),
            pltpu.SemaphoreType.DMA((5,)),
            pltpu.SemaphoreType.DMA((4,)),
            pltpu.SemaphoreType.DMA((6, n - 1)),
            pltpu.SemaphoreType.DMA((6, n - 1)),
        ],
        compiler_params=pltpu.CompilerParams(
            collective_id=0, has_side_effects=True, vmem_limit_bytes=63 * 2**20
        ),
    )(
        genotype,
        allele_freq.reshape(1, -1),
        person_weight.reshape(-1, TILE),
        basis,
        residuals,
        block_markers.reshape(1, -1),
    )
    return pl.pallas_call(
        write_results,
        out_shape=shapes,
        in_specs=[hbm] * 4,
        out_specs=(hbm,) * 4,
        scratch_shapes=[pltpu.VMEM(shape.shape, shape.dtype) for shape in shapes]
        + [pltpu.SemaphoreType.DMA((4,))] * 2,
    )(*results)


def solution(mesh):
    small = mesh.shape["people"] == 4 and mesh.shape["markers"] == 4
    placed = (
        P(("cohort", "people"), "markers"),
        P(("cohort", "markers")),
        P(("cohort", "people")),
        P("cohort", "markers"),
        P("cohort", "people"),
        P("markers"),
    )
    return jax.shard_map(
        fused if small else shards,
        mesh=mesh,
        in_specs=placed,
        out_specs=(
            P("cohort", "people"),
            P("cohort", None),
            P("markers", "cohort", "people"),
            P("markers", "cohort", "people"),
        ),
        check_vma=False,
    )
```

profile of v0, /device:TPU:0, one launch (start us, length us, event | category | flops | bytes accessed | tf_op | source)
XLA Modules:
  0.0 29.3 jit_solution(7709927283586745565)
XLA Ops:
  0.6 27.0 %shard_map.93 = (f32[32,1536]{1,0:T(8,128)}, f32[32,64]{1,0:T(8,128)}, f32[1,32,512]{2,1,0:T(8,128)}, f32[1,64,128]{2,1,0:T(8,128)}) custom-call(s32[1536,512]{1,0:T(8,128)} %geno_hbm.1, f32[1,2048]{1,0:T(1,128)} %bitcast.3, f32[12,128]{1,0:T(8,128)} %bitcast.4, bf16[32,2048]{1,0:T(8,128)(2,1)} %basis_hbm.1, bf16[64,1536]{1,0:T(8,128)(2,1)} %resid_hbm.1, ...), custom_call_target="tpu_custom_call" | custom-call | tf_op jit(solution)/shard_map/pallas_call | solution.py:423
  27.6 1.7 %shard_map.94 = (f32[32,1536]{1,0:T(8,128)}, f32[32,64]{1,0:T(8,128)}, f32[1,32,512]{2,1,0:T(8,128)}, f32[1,64,128]{2,1,0:T(8,128)}) custom-call(f32[32,1536]{1,0:T(8,128)} %get-tuple-element.8.refs_0_, f32[32,64]{1,0:T(8,128)} %get-tuple-element.9.refs_1_, f32[1,32,512]{2,1,0:T(8,128)} %get-tuple-element.10.refs_2_, f32[1,64,128]{2,1,0:T(8,128)} %get-tuple-element.11.refs_3_), custom_call_target="tpu_custom_call" | custom-call | tf_op jit(solution)/shard_map/pallas_call | solution.py:471
where the time goes:
time: 29.5 us; the launch traced here: 29.3 us
  Pallas kernels  28.7 us (97%)
  between operations  0.64 us (2%)
    pallas_call x1, Pallas kernels, fused(): pl.pallas_call(functools.partial(kernel, root_people), out_shape=shapes,...  27 us
    pallas_call x1, Pallas kernels, fused(): pl.pallas_call(write_results, out_shape=shapes, in_specs=[hbm] * 4, out_s...  1.7 us

commit v1 on v0

--- a/solution.py
+++ b/solution.py
@@ -132,10 +132,6 @@
     basis_hbm,
     resid_hbm,
     block_hbm,
-    comp_hbm,
-    coef_hbm,
-    next_hbm,
-    score_hbm,
     comp_ref,
     coef_ref,
     next_ref,
@@ -163,7 +159,6 @@
     chosen_in,
     geno_sem,
     load_sem,
-    store_sem,
     send_sem,
     recv_sem,
 ):
@@ -345,19 +340,6 @@
     comp_ref[...] = root_people * jnp.dot(
         inverse, sketch, preferred_element_type=jnp.float32, precision=lax.Precision.HIGHEST
     )
-    stores = [
-        pltpu.make_async_copy(src, dst, store_sem.at[i])
-        for i, (src, dst) in enumerate(
-            (
-                (coef_ref, coef_hbm),
-                (comp_ref, comp_hbm),
-                (next_ref, next_hbm),
-                (score_ref, score_hbm),
-            )
-        )
-    ]
-    stores[0].start()
-    stores[1].start()
 
     for d in range(1, n):
         sends[2, d].wait_recv()
@@ -373,7 +355,6 @@
         precision=lax.Precision.HIGHEST,
     )
     next_ref[0] = sum3(mm_nt(split3(solved[:, :block]), perm[...]))
-    stores[2].start()
     removed = lax.dot_general(
         coef,
         solved[:, block:],
@@ -382,21 +363,14 @@
         precision=lax.Precision.HIGHEST,
     )
     score_ref[0] = (scored - removed) * (1.0 / root_people)
-    stores[3].start()
-    for store in stores:
-        store.wait()
     for copy in sends.values():
         copy.wait_send()
 
 
 def write_results(*refs):
-    sources, results, held, (load_sem, store_sem) = refs[:4], refs[4:8], refs[8:12], refs[12:]
-    loads = [pltpu.make_async_copy(sources[i], held[i], load_sem.at[i]) for i in range(4)]
-    stores = [pltpu.make_async_copy(held[i], results[i], store_sem.at[i]) for i in range(4)]
-    for load in loads:
-        load.start()
-    for load, store in zip(loads, stores):
-        load.wait()
+    sources, results, store_sem = refs[:4], refs[4:8], refs[8]
+    stores = [pltpu.make_async_copy(sources[i], results[i], store_sem.at[i]) for i in range(4)]
+    for store in stores:
         store.start()
     for store in stores:
         store.wait()
@@ -413,6 +387,7 @@
     width = picks // n
     f32, bf16 = jnp.float32, jnp.bfloat16
     hbm = pl.BlockSpec(memory_space=pltpu.HBM)
+    vmem = pl.BlockSpec(memory_space=pltpu.VMEM)
     root_people = math.sqrt(rows * n)
     shapes = (
         jax.ShapeDtypeStruct((k_count, rows), f32),
@@ -422,14 +397,10 @@
     )
     results = pl.pallas_call(
         functools.partial(kernel, root_people),
-        out_shape=shapes,
+        out_shape=tuple(pltpu.VMEM(shape.shape, shape.dtype) for shape in shapes),
         in_specs=[hbm] * 6,
-        out_specs=(hbm,) * 4,
+        out_specs=(vmem,) * 4,
         scratch_shapes=[
-            pltpu.VMEM((k_count, rows), f32),
-            pltpu.VMEM((k_count, r_count), f32),
-            pltpu.VMEM((1, k_count, block), f32),
-            pltpu.VMEM((1, r_count, width), f32),
             pltpu.VMEM((rows, words), jnp.int32),
             pltpu.VMEM((1, n * block), f32),
             pltpu.VMEM((rows // TILE, TILE), f32),
@@ -453,12 +424,11 @@
             pltpu.VMEM((n - 1, k_count, width), f32),
             pltpu.SemaphoreType.DMA((n,)),
             pltpu.SemaphoreType.DMA((5,)),
-            pltpu.SemaphoreType.DMA((4,)),
             pltpu.SemaphoreType.DMA((6, n - 1)),
             pltpu.SemaphoreType.DMA((6, n - 1)),
         ],
         compiler_params=pltpu.CompilerParams(
-            collective_id=0, has_side_effects=True, vmem_limit_bytes=63 * 2**20
+            collective_id=0, has_side_effects=True, vmem_limit_bytes=62 * 2**20
         ),
     )(
         genotype,
@@ -471,11 +441,10 @@
     return pl.pallas_call(
         write_results,
         out_shape=shapes,
-        in_specs=[hbm] * 4,
+        in_specs=[vmem] * 4,
         out_specs=(hbm,) * 4,
-        scratch_shapes=[pltpu.VMEM(shape.shape, shape.dtype) for shape in shapes]
-        + [pltpu.SemaphoreType.DMA((4,))] * 2,
-    )(*results)
+        scratch_shapes=[pltpu.SemaphoreType.DMA((4,))],
+    )(*[pltpu.with_memory_space_constraint(r, pltpu.VMEM) for r in results])
 
 
 def solution(mesh):

time: 29.5 us -> 27.9 us (0.946)
  Pallas kernels: 28.7 us -> 27.1 us
    pallas_call x2, Pallas kernels: 28.7 us -> 27.1 us  [the longest x1 26.3 us: fused(): pl.pallas_call(functools.partial(kernel, root_people), out_shape=tuple((p...]
where the time goes in v1:
time: 27.9 us; the launch traced here: 27.7 us
  Pallas kernels  27.1 us (97%)
  between operations  0.64 us (2%)
    pallas_call x1, Pallas kernels, fused(): pl.pallas_call(functools.partial(kernel, root_people), out_shape=tuple((p...  26.3 us
    pallas_call x1, Pallas kernels, fused(): pl.pallas_call(write_results, out_shape=shapes, in_specs=[vmem] * 4, out_...  0.74 us

profile of v1, /device:TPU:0, one launch (start us, length us, event | category | flops | bytes accessed | tf_op | source)
XLA Modules:
  0.0 27.7 jit_solution(476854024446427782)
XLA Ops:
  0.6 26.3 %shard_map.93 = (f32[32,1536]{1,0:T(8,128)S(1)}, f32[32,64]{1,0:T(8,128)S(1)}, f32[1,32,512]{2,1,0:T(8,128)S(1)}, f32[1,64,128]{2,1,0:T(8,128)S(1)}) custom-call(s32[1536,512]{1,0:T(8,128)} %geno_hbm.1, f32[1,2048]{1,0:T(1,128)} %bitcast.3, f32[12,128]{1,0:T(8,128)} %bitcast.4, bf16[32,2048]{1,0:T(8,128)(2,1)} %basis_hbm.1, bf16[64,1536]{1,0:T(8,128)(2,1)} %resid_hbm.1, ...), custom_call_target="tpu_custom_call" | custom-call | tf_op jit(solution)/shard_map/pallas_call | solution.py:398
  27.0 0.7 %shard_map.94 = (f32[32,1536]{1,0:T(8,128)}, f32[32,64]{1,0:T(8,128)}, f32[1,32,512]{2,1,0:T(8,128)}, f32[1,64,128]{2,1,0:T(8,128)}) custom-call(f32[32,1536]{1,0:T(8,128)S(1)} %get-tuple-element.8.refs_0_, f32[32,64]{1,0:T(8,128)S(1)} %get-tuple-element.9.refs_1_, f32[1,32,512]{2,1,0:T(8,128)S(1)} %get-tuple-element.10.refs_2_, ...), custom_call_target="tpu_custom_call" | custom-call | tf_op jit(solution)/shard_map/pallas_call | solution.py:441

commit v2 on v1

--- a/solution.py
+++ b/solution.py
@@ -82,8 +82,14 @@
     return (components, coefficients, basis_own[None], scores)
 
 
-ROWS_STEP = 128
 TILE = 128
+PIECES = (512, 512, 256, 256)
+
+
+def split2(value):
+    first = value.astype(jnp.bfloat16)
+    second = (value - first.astype(jnp.float32)).astype(jnp.bfloat16)
+    return jnp.concatenate([first, second], axis=0)
 
 
 def split3(value):
@@ -94,6 +100,11 @@
     return jnp.concatenate([first, second, third], axis=0)
 
 
+def sum2(value):
+    half = value.shape[0] // 2
+    return value[:half] + value[half:]
+
+
 def sum3(value):
     third = value.shape[0] // 3
     return value[:third] + value[third : 2 * third] + value[2 * third :]
@@ -103,13 +114,15 @@
     return jnp.dot(left, right, preferred_element_type=jnp.float32)
 
 
-def mm_nt(left, right, precision=None):
+def mm_nt(left, right):
     return lax.dot_general(
-        left,
-        right,
-        (((1,), (1,)), ((), ())),
-        preferred_element_type=jnp.float32,
-        precision=precision,
+        left, right, (((1,), (1,)), ((), ())), preferred_element_type=jnp.float32
+    )
+
+
+def exact(left, right):
+    return jnp.dot(
+        left, right, preferred_element_type=jnp.float32, precision=lax.Precision.HIGHEST
     )
 
 
@@ -142,14 +155,16 @@
     basis_ref,
     resid_ref,
     block_ref,
-    wt,
+    dose,
     hot,
     perm,
     freq_rows,
     basis_rows,
     part,
-    part_in,
-    sketch_all,
+    core_in,
+    chip_part,
+    chip_in,
+    sketch_half,
     resid_score,
     resid_score_in,
     gram_all,
@@ -159,120 +174,146 @@
     chosen_in,
     geno_sem,
     load_sem,
+    pair_send,
+    pair_recv,
     send_sem,
     recv_sem,
 ):
     people = lax.axis_index("people")
     markers = lax.axis_index("markers")
     n = 4
-    k_count, share = part.shape[1], part.shape[2]
-    block = wt.shape[2]
+    half = part.shape[1]
+    k_count = 2 * half
+    block = dose.shape[2]
     words = block // 4
-    marker_peer = [lax.rem(markers + d, n) for d in range(n)]
-    people_peer = [lax.rem(people + d, n) for d in range(n)]
-    order = [1, 2, 3, 0]
-
-    small = []
-    for i, (src, dst) in enumerate(
-        (
-            (freq_hbm, freq_ref),
-            (basis_hbm, basis_ref),
-            (weight_hbm, weight_ref),
-            (block_hbm, block_ref),
-            (resid_hbm, resid_ref),
+    core = lax.rem(markers, 2)
+    core_peer = markers + 1 - 2 * core
+    chip_peer = lax.rem(markers + 2, n)
+    people_peer = [people, people + 1 - 2 * lax.rem(people, 2), lax.rem(people + 2, n), 3 - people]
+    starts = [sum(PIECES[:i]) for i in range(len(PIECES))]
+    spans = [pl.ds(start, size) for start, size in zip(starts, PIECES)]
+
+    loads = []
+    for i, span in enumerate(spans):
+        loads.append(pltpu.make_async_copy(geno_hbm.at[span], geno.at[span], geno_sem.at[i]))
+    small = [
+        pltpu.make_async_copy(src, dst, load_sem.at[i])
+        for i, (src, dst) in enumerate(
+            (
+                (freq_hbm, freq_ref),
+                (basis_hbm, basis_ref),
+                (weight_hbm, weight_ref),
+                (block_hbm, block_ref),
+                (resid_hbm, resid_ref),
+            )
         )
-    ):
-        small.append(pltpu.make_async_copy(src, dst, load_sem.at[i]))
-        small[-1].start()
-    for step, d in enumerate(order):
-        at = pl.ds(pl.multiple_of(marker_peer[d] * share, share), share)
-        pltpu.make_async_copy(geno_hbm.at[at], geno.at[at], geno_sem.at[step]).start()
+    ]
+    for load in small[:3] + loads + small[3:]:
+        load.start()
 
     barrier = pltpu.get_barrier_semaphore()
-    for d in range(1, n):
-        pl.semaphore_signal(
-            barrier, inc=1, device_id={"markers": marker_peer[d]}, device_id_type=MESH
-        )
+    for peer in (core_peer, chip_peer):
+        pl.semaphore_signal(barrier, inc=1, device_id={"markers": peer}, device_id_type=MESH)
+    for d in (1, 2, 3):
         pl.semaphore_signal(
             barrier, inc=1, device_id={"people": people_peer[d]}, device_id_type=MESH
         )
 
     sends = {}
 
-    def send(group, d, src, dst, axis):
-        peer = marker_peer[d] if axis == "markers" else people_peer[d]
+    def send(group, d, src, dst):
         copy = pltpu.make_async_remote_copy(
             src_ref=src,
             dst_ref=dst,
             send_sem=send_sem.at[group, d - 1],
             recv_sem=recv_sem.at[group, d - 1],
-            device_id={axis: peer},
+            device_id={"people": people_peer[d]},
             device_id_type=MESH,
         )
         copy.start()
         sends[group, d] = copy
 
+    pairs = {}
+
+    def pair(level, i):
+        src, dst, peer = (
+            (part.at[1 - core], core_in, core_peer),
+            (chip_part, chip_in, chip_peer),
+            (sketch_half.at[core], sketch_half.at[core], core_peer),
+        )[level]
+        copy = pltpu.make_async_remote_copy(
+            src_ref=src.at[:, spans[i]],
+            dst_ref=dst.at[:, spans[i]],
+            send_sem=pair_send.at[level, i],
+            recv_sem=pair_recv.at[level, i],
+            device_id={"markers": peer},
+            device_id_type=MESH,
+        )
+        copy.start()
+        pairs[level, i] = copy
+
+    place = lax.broadcasted_iota(jnp.int32, (1, block), 1)
+    source = 4 * lax.rem(place, words) + lax.div(place, words)
     marker = lax.broadcasted_iota(jnp.int32, (block, block), 0)
-    place = lax.broadcasted_iota(jnp.int32, (block, block), 1)
-    perm[...] = jnp.where(
-        marker == 4 * lax.rem(place, words) + lax.div(place, words), 1.0, 0.0
-    ).astype(jnp.bfloat16)
+    perm[...] = jnp.where(marker == source, 1.0, 0.0).astype(jnp.bfloat16)
     small[0].wait()
     small[1].wait()
     small[2].wait()
     freq = jnp.concatenate([freq_ref[:, c * block : (c + 1) * block] for c in range(n)], axis=0)
     freq = jnp.concatenate([freq, freq], axis=0)
     freq = sum3(mm(split3(freq), perm[...]))[:n]
-    freq_rows[0:n, :] = 2.0 * freq
-    freq_rows[n : 2 * n, :] = 1.0 / jnp.sqrt(2.0 * freq * (1.0 - freq))
+    twice = 2.0 * freq
+    scale = 1.0 / jnp.sqrt(2.0 * freq * (1.0 - freq))
+    freq_rows[0:n, :] = twice
+    freq_rows[n : 2 * n, :] = scale
     basis = jnp.concatenate([basis_ref[:, c * block : (c + 1) * block] for c in range(n)], axis=0)
-    basis_rows[...] = mm(basis, perm[...]).astype(jnp.bfloat16)
-
-    pl.semaphore_wait(barrier, 2 * (n - 1))
-
-    def share_copy(slot, target):
-        return pltpu.make_async_remote_copy(
-            src_ref=part.at[target],
-            dst_ref=part_in.at[slot],
-            send_sem=send_sem.at[0, slot],
-            recv_sem=recv_sem.at[0, slot],
-            device_id={"markers": target},
-            device_id_type=MESH,
+    basis = mm(basis, perm[...])
+    offset = jnp.zeros((k_count, 1), jnp.float32)
+    for c in range(n):
+        scaled = split2(basis[c * k_count : (c + 1) * k_count] * scale[c : c + 1])
+        basis_rows[c] = scaled
+        offset += jnp.sum(
+            sum2(scaled.astype(jnp.float32)) * twice[c : c + 1], axis=1, keepdims=True
         )
-
-    def decode(step, carry):
-        target = lax.rem(markers + step + 1, n)
-        at = pl.ds(pl.multiple_of(target * share, share), share)
-        pltpu.make_async_copy(geno_hbm.at[at], geno.at[at], geno_sem.at[step]).wait()
-        weight = []
-        for i in range(share // ROWS_STEP):
-            line = weight_ref[pl.ds(target * (share // ROWS_STEP) + i, 1), :]
-            weight.append(jnp.transpose(jnp.broadcast_to(line, (ROWS_STEP, TILE))))
-        weight = jnp.concatenate(weight, axis=0)
+    weight = jnp.concatenate(
+        [weight_ref[i : i + 1, :] for i in range(weight_ref.shape[0])], axis=1
+    )
+
+    pl.semaphore_wait(barrier, 5)
+
+    def forward(i):
+        pairs[0, i].wait_recv()
+        chip_part[:, spans[i]] = part[core, :, spans[i]] + core_in[:, spans[i]]
+        pair(1, i)
+
+    def finish(i):
+        pairs[1, i].wait_recv()
+        sketch_half[core, :, spans[i]] = chip_part[:, spans[i]] + chip_in[:, spans[i]]
+        pair(2, i)
+
+    for i, span in enumerate(spans):
+        loads[i].wait()
         total = None
         for c in range(n):
-            packed = geno[at, c * words : (c + 1) * words]
-            tiles = []
-            for j in range(4):
-                cols = slice(j * words, (j + 1) * words)
-                dosage = jnp.bitwise_and(jnp.right_shift(packed, 2 * j), 3).astype(jnp.float32)
-                value = (dosage - freq_rows[c : c + 1, cols]) * freq_rows[n + c : n + c + 1, cols]
-                tiles.append((weight * value).astype(jnp.bfloat16))
-            tile = jnp.concatenate(tiles, axis=1)
-            wt[c, at, :] = tile
-            got = mm_nt(basis_rows[c * k_count : (c + 1) * k_count, :], tile)
+            packed = geno[span, c * words : (c + 1) * words]
+            tile = jnp.concatenate(
+                [
+                    jnp.bitwise_and(jnp.right_shift(packed, 2 * j), 3)
+                    .astype(jnp.float32)
+                    .astype(jnp.bfloat16)
+                    for j in range(4)
+                ],
+                axis=1,
+            )
+            dose[c, span, :] = tile
+            got = mm_nt(basis_rows[c], tile)
             total = got if total is None else total + got
-        part[target] = total
-
-        @pl.when(step < n - 1)
-        def _():
-            share_copy(step, target).start()
-
-        return carry
-
-    lax.fori_loop(0, n, decode, 0)
-    for d in range(1, n):
-        sends[0, d] = share_copy(d - 1, marker_peer[d])
+        value = (sum2(total) - offset) * weight[:, starts[i] : starts[i] + PIECES[i]]
+        part[0, :, span] = value[:half]
+        part[1, :, span] = value[half:]
+        pair(0, i)
+        if i:
+            forward(i - 1)
 
     small[3].wait()
     small[4].wait()
@@ -282,53 +323,62 @@
     for c in range(n):
         row = lax.broadcasted_iota(jnp.int32, (block, hot.shape[2]), 0) + c * block
         hot[c] = jnp.where(row == column, 1.0, 0.0).astype(jnp.bfloat16)
-
-    for d in range(1, n):
-        sends[0, d].wait_recv()
-    sketch_all[markers] = part[markers] + part_in[0] + part_in[1] + part_in[2]
-    for d in range(1, n):
-        send(1, d, sketch_all.at[markers], sketch_all.at[markers], "markers")
+    forward(len(PIECES) - 1)
+
+    def center(raw, sums, c):
+        return (raw - sums * freq_rows[c : c + 1, :]) * freq_rows[n + c : n + c + 1, :]
 
     resid = resid_ref[...]
+    heavy = split2(resid.astype(jnp.float32) * weight)
+    sums = sum2(jnp.sum(heavy.astype(jnp.float32), axis=1, keepdims=True))
     picked = None
     for c in range(n):
-        got = mm(split3(mm(resid, wt[c])), hot[c])
+        value = center(sum2(mm(heavy, dose[c])), sums, c)
+        got = mm(split2(value), hot[c])
         picked = got if picked is None else picked + got
-    picked = sum3(picked)
+    picked = sum2(picked)
     width = picked.shape[1] // n
     for c in range(n):
         resid_score[c] = picked[:, c * width : (c + 1) * width]
-    for d in range(1, n):
-        send(2, d, resid_score.at[people_peer[d]], resid_score_in.at[d - 1], "people")
-
-    for d in range(1, n):
-        sends[1, d].wait_recv()
-    sketch = jnp.concatenate([sketch_all[c] for c in range(n)], axis=1)
-    both = jnp.concatenate([sketch, resid.astype(jnp.float32)], axis=0)
-    gram = mm_nt(sketch, both, lax.Precision.HIGHEST)
-    pad = jnp.zeros((k_count, TILE - gram.shape[1]), jnp.float32)
-    gram_all[people] = jnp.concatenate([gram, pad], axis=1)
-    for d in range(1, n):
-        send(3, d, gram_all.at[people], gram_all.at[people], "people")
-
+    for d in (2, 3, 1):
+        send(0, d, resid_score.at[people_peer[d]], resid_score_in.at[d - 1])
+
+    for i in range(len(PIECES)):
+        finish(i)
+    for i in range(len(PIECES)):
+        pairs[2, i].wait_recv()
+    sketch = jnp.concatenate([sketch_half[0], sketch_half[1]], axis=0)
     pieces = split3(sketch)
+    gram = sum3(mm_nt(pieces, jnp.concatenate([pieces, resid], axis=0)))
+    square = (
+        gram[:, :k_count] + gram[:, k_count : 2 * k_count] + gram[:, 2 * k_count : 3 * k_count]
+    )
+    pad = jnp.zeros((k_count, k_count), jnp.float32)
+    gram_all[people] = jnp.concatenate([square, gram[:, 3 * k_count :], pad], axis=1)
+    for d in (2, 3, 1):
+        send(1, d, gram_all.at[people], gram_all.at[people])
+
+    heavy = split2(sketch * weight)
+    sums = sum2(jnp.sum(heavy.astype(jnp.float32), axis=1, keepdims=True))
     picked = None
-    for d in (2, 1, 3, 0):
+    for d in (2, 3, 1, 0):
         c = people_peer[d]
-        total = sum3(mm(pieces, wt[c]))
+        freq_row = freq_rows[pl.ds(c, 1), :]
+        scale_row = freq_rows[pl.ds(c + n, 1), :]
+        total = (sum2(mm(heavy, dose[c])) - sums * freq_row) * scale_row
         next_part[c] = total
         if d:
-            send(4, d, next_part.at[c], next_in.at[d - 1], "people")
-        got = mm(split3(total), hot[c])
+            send(2, d, next_part.at[c], next_in.at[d - 1])
+        got = mm(split2(total), hot[c])
         picked = got if picked is None else picked + got
-    picked = sum3(picked)
+    picked = sum2(picked)
     for c in range(n):
         chosen_part[c] = picked[:, c * width : (c + 1) * width]
-    for d in range(1, n):
-        send(5, d, chosen_part.at[people_peer[d]], chosen_in.at[d - 1], "people")
-
-    for d in range(1, n):
-        sends[3, d].wait_recv()
+    for d in (2, 3, 1):
+        send(3, d, chosen_part.at[people_peer[d]], chosen_in.at[d - 1])
+
+    for d in (1, 2, 3):
+        sends[1, d].wait_recv()
     full = gram_all[0] + gram_all[1] + gram_all[2] + gram_all[3]
     lane = lax.broadcasted_iota(jnp.int32, full.shape, 1)
     line = lax.broadcasted_iota(jnp.int32, full.shape, 0)
@@ -337,33 +387,25 @@
     coef = full[:, k_count : TILE - k_count]
     inverse = full[:, TILE - k_count :]
     coef_ref[...] = coef
-    comp_ref[...] = root_people * jnp.dot(
-        inverse, sketch, preferred_element_type=jnp.float32, precision=lax.Precision.HIGHEST
-    )
-
-    for d in range(1, n):
-        sends[2, d].wait_recv()
-        sends[4, d].wait_recv()
-        sends[5, d].wait_recv()
+    comp_ref[...] = root_people * exact(inverse, sketch)
+    remover = lax.dot_general(
+        coef,
+        inverse,
+        (((0,), (0,)), ((), ())),
+        preferred_element_type=jnp.float32,
+        precision=lax.Precision.HIGHEST,
+    )
+
+    for group in (0, 2, 3):
+        for d in (1, 2, 3):
+            sends[group, d].wait_recv()
     total = next_part[people] + next_in[0] + next_in[1] + next_in[2]
     chosen = chosen_part[people] + chosen_in[0] + chosen_in[1] + chosen_in[2]
     scored = resid_score[people] + resid_score_in[0] + resid_score_in[1] + resid_score_in[2]
-    solved = jnp.dot(
-        inverse,
-        jnp.concatenate([total, chosen], axis=1),
-        preferred_element_type=jnp.float32,
-        precision=lax.Precision.HIGHEST,
-    )
-    next_ref[0] = sum3(mm_nt(split3(solved[:, :block]), perm[...]))
-    removed = lax.dot_general(
-        coef,
-        solved[:, block:],
-        (((0,), (0,)), ((), ())),
-        preferred_element_type=jnp.float32,
-        precision=lax.Precision.HIGHEST,
-    )
-    score_ref[0] = (scored - removed) * (1.0 / root_people)
-    for copy in sends.values():
+    solved = exact(inverse, total)
+    next_ref[0] = sum3(mm_nt(split3(solved), perm[...]))
+    score_ref[0] = (scored - exact(remover, chosen)) * (1.0 / root_people)
+    for copy in list(pairs.values()) + list(sends.values()):
         copy.wait_send()
 
 
@@ -381,7 +423,6 @@
     rows, words = genotype.shape
     k_count = basis.shape[0]
     r_count = residuals.shape[0]
-    share = rows // n
     block = 4 * words // n
     picks = block_markers.shape[0]
     width = picks // n
@@ -411,10 +452,12 @@
             pltpu.VMEM((n, block, picks), bf16),
             pltpu.VMEM((block, block), bf16),
             pltpu.VMEM((2 * n, block), f32),
-            pltpu.VMEM((n * k_count, block), bf16),
-            pltpu.VMEM((n, k_count, share), f32),
-            pltpu.VMEM((n - 1, k_count, share), f32),
-            pltpu.VMEM((n, k_count, share), f32),
+            pltpu.VMEM((n, 2 * k_count, block), bf16),
+            pltpu.VMEM((2, k_count // 2, rows), f32),
+            pltpu.VMEM((k_count // 2, rows), f32),
+            pltpu.VMEM((k_count // 2, rows), f32),
+            pltpu.VMEM((k_count // 2, rows), f32),
+            pltpu.VMEM((2, k_count // 2, rows), f32),
             pltpu.VMEM((n, r_count, width), f32),
             pltpu.VMEM((n - 1, r_count, width), f32),
             pltpu.VMEM((n, k_count, TILE), f32),
@@ -422,10 +465,12 @@
             pltpu.VMEM((n - 1, k_count, block), f32),
             pltpu.VMEM((n, k_count, width), f32),
             pltpu.VMEM((n - 1, k_count, width), f32),
-            pltpu.SemaphoreType.DMA((n,)),
+            pltpu.SemaphoreType.DMA((len(PIECES),)),
             pltpu.SemaphoreType.DMA((5,)),
-            pltpu.SemaphoreType.DMA((6, n - 1)),
-            pltpu.SemaphoreType.DMA((6, n - 1)),
+            pltpu.SemaphoreType.DMA((3, len(PIECES))),
+            pltpu.SemaphoreType.DMA((3, len(PIECES))),
+            pltpu.SemaphoreType.DMA((4, n - 1)),
+            pltpu.SemaphoreType.DMA((4, n - 1)),
         ],
         compiler_params=pltpu.CompilerParams(
             collective_id=0, has_side_effects=True, vmem_limit_bytes=62 * 2**20

time: 27.9 us -> 25.7 us (0.921)
  Pallas kernels: 27.1 us -> 24.9 us
    pallas_call x1, Pallas kernels: 26.3 us -> 24.2 us  [fused(): pl.pallas_call(functools.partial(kernel, root_people), out_shape=tuple((p...]
where the time goes in v2:
time: 25.7 us; the launch traced here: 25.5 us
  Pallas kernels  24.9 us (97%)
  between operations  0.64 us (2%)
    pallas_call x1, Pallas kernels, fused(): pl.pallas_call(functools.partial(kernel, root_people), out_shape=tuple((p...  24.2 us
    pallas_call x1, Pallas kernels, fused(): pl.pallas_call(write_results, out_shape=shapes, in_specs=[vmem] * 4, out_...  0.74 us

profile of v2, /device:TPU:0, one launch (start us, length us, event | category | flops | bytes accessed | tf_op | source)
XLA Modules:
  0.0 25.5 jit_solution(1288852339181748023)
XLA Ops:
  0.6 24.2 %shard_map.93 = (f32[32,1536]{1,0:T(8,128)S(1)}, f32[32,64]{1,0:T(8,128)S(1)}, f32[1,32,512]{2,1,0:T(8,128)S(1)}, f32[1,64,128]{2,1,0:T(8,128)S(1)}) custom-call(s32[1536,512]{1,0:T(8,128)} %geno_hbm.1, f32[1,2048]{1,0:T(1,128)} %bitcast.3, f32[12,128]{1,0:T(8,128)} %bitcast.4, bf16[32,2048]{1,0:T(8,128)(2,1)} %basis_hbm.1, bf16[64,1536]{1,0:T(8,128)(2,1)} %resid_hbm.1, ...), custom_call_target="tpu_custom_call" | custom-call | tf_op jit(solution)/shard_map/pallas_call | solution.py:439
  24.8 0.7 %shard_map.94 = (f32[32,1536]{1,0:T(8,128)}, f32[32,64]{1,0:T(8,128)}, f32[1,32,512]{2,1,0:T(8,128)}, f32[1,64,128]{2,1,0:T(8,128)}) custom-call(f32[32,1536]{1,0:T(8,128)S(1)} %get-tuple-element.8.refs_0_, f32[32,64]{1,0:T(8,128)S(1)} %get-tuple-element.9.refs_1_, f32[1,32,512]{2,1,0:T(8,128)S(1)} %get-tuple-element.10.refs_2_, ...), custom_call_target="tpu_custom_call" | custom-call | tf_op jit(solution)/shard_map/pallas_call | solution.py:486

commit v3 on v2

--- a/solution.py
+++ b/solution.py
@@ -167,11 +167,20 @@
     sketch_half,
     resid_score,
     resid_score_in,
-    gram_all,
+    gram_part,
+    gram_in,
+    gram_sum,
     next_part,
+    next_near,
     next_in,
+    next_mine,
+    next_pass,
+    next_far,
     chosen_part,
-    chosen_in,
+    chosen_near,
+    chosen_mine,
+    chosen_pass,
+    chosen_far,
     geno_sem,
     load_sem,
     pair_send,
@@ -225,9 +234,9 @@
         copy = pltpu.make_async_remote_copy(
             src_ref=src,
             dst_ref=dst,
-            send_sem=send_sem.at[group, d - 1],
-            recv_sem=recv_sem.at[group, d - 1],
-            device_id={"people": people_peer[d]},
+            send_sem=send_sem.at[group, d],
+            recv_sem=recv_sem.at[group, d],
+            device_id={"people": people_peer[d]} if d else {"markers": core_peer},
             device_id_type=MESH,
         )
         copy.start()
@@ -270,10 +279,10 @@
     basis = mm(basis, perm[...])
     offset = jnp.zeros((k_count, 1), jnp.float32)
     for c in range(n):
-        scaled = split2(basis[c * k_count : (c + 1) * k_count] * scale[c : c + 1])
+        scaled = (basis[c * k_count : (c + 1) * k_count] * scale[c : c + 1]).astype(jnp.bfloat16)
         basis_rows[c] = scaled
         offset += jnp.sum(
-            sum2(scaled.astype(jnp.float32)) * twice[c : c + 1], axis=1, keepdims=True
+            scaled.astype(jnp.float32) * twice[c : c + 1], axis=1, keepdims=True
         )
     weight = jnp.concatenate(
         [weight_ref[i : i + 1, :] for i in range(weight_ref.shape[0])], axis=1
@@ -308,7 +317,7 @@
             dose[c, span, :] = tile
             got = mm_nt(basis_rows[c], tile)
             total = got if total is None else total + got
-        value = (sum2(total) - offset) * weight[:, starts[i] : starts[i] + PIECES[i]]
+        value = (total - offset) * weight[:, starts[i] : starts[i] + PIECES[i]]
         part[0, :, span] = value[:half]
         part[1, :, span] = value[half:]
         pair(0, i)
@@ -348,38 +357,57 @@
     for i in range(len(PIECES)):
         pairs[2, i].wait_recv()
     sketch = jnp.concatenate([sketch_half[0], sketch_half[1]], axis=0)
-    pieces = split3(sketch)
-    gram = sum3(mm_nt(pieces, jnp.concatenate([pieces, resid], axis=0)))
-    square = (
-        gram[:, :k_count] + gram[:, k_count : 2 * k_count] + gram[:, 2 * k_count : 3 * k_count]
-    )
-    pad = jnp.zeros((k_count, k_count), jnp.float32)
-    gram_all[people] = jnp.concatenate([square, gram[:, 3 * k_count :], pad], axis=1)
-    for d in (2, 3, 1):
-        send(1, d, gram_all.at[people], gram_all.at[people])
-
     heavy = split2(sketch * weight)
     sums = sum2(jnp.sum(heavy.astype(jnp.float32), axis=1, keepdims=True))
+    cut = block // 2
     picked = None
-    for d in (2, 3, 1, 0):
+    for d in (3, 2, 1, 0):
         c = people_peer[d]
         freq_row = freq_rows[pl.ds(c, 1), :]
         scale_row = freq_rows[pl.ds(c + n, 1), :]
         total = (sum2(mm(heavy, dose[c])) - sums * freq_row) * scale_row
-        next_part[c] = total
-        if d:
-            send(2, d, next_part.at[c], next_in.at[d - 1])
+        next_part[c, 0] = total[:, :cut]
+        next_part[c, 1] = total[:, cut:]
+        if d == 3:
+            send(2, 1, next_part.at[c, 1], next_pass)
+        if d > 1:
+            send(2, d, next_part.at[c, 0], next_in.at[d - 2])
         got = mm(split2(total), hot[c])
         picked = got if picked is None else picked + got
+        if d == 3:
+            pieces = split3(sketch)
+            gram = sum3(mm_nt(pieces, jnp.concatenate([pieces, resid], axis=0)))
+            square = (
+                gram[:, :k_count]
+                + gram[:, k_count : 2 * k_count]
+                + gram[:, 2 * k_count : 3 * k_count]
+            )
+            pad = jnp.zeros((k_count, k_count), jnp.float32)
+            gram = jnp.concatenate([square, gram[:, 3 * k_count :], pad], axis=1)
+            gram_part[0] = gram[:half]
+            gram_part[1] = gram[half:]
+            gram_in[people] = gram_part[core]
+            for far in (3, 2, 1):
+                send(1, far, gram_part.at[core], gram_in.at[people])
     picked = sum2(picked)
     for c in range(n):
         chosen_part[c] = picked[:, c * width : (c + 1) * width]
-    for d in (2, 3, 1):
-        send(3, d, chosen_part.at[people_peer[d]], chosen_in.at[d - 1])
-
+    send(4, 1, chosen_part.at[people_peer[3]], chosen_pass)
+    send(5, 1, chosen_part.at[people_peer[1]], chosen_near)
+
+    sends[2, 1].wait_recv()
+    next_mine[...] = next_part[people_peer[2], 1] + next_pass[...]
+    send(3, 2, next_mine, next_far)
+    send(3, 1, next_part.at[people_peer[1]], next_near)
     for d in (1, 2, 3):
         sends[1, d].wait_recv()
-    full = gram_all[0] + gram_all[1] + gram_all[2] + gram_all[3]
+    gram_sum[core] = gram_in[0] + gram_in[1] + gram_in[2] + gram_in[3]
+    send(1, 0, gram_sum.at[core], gram_sum.at[core])
+    sends[4, 1].wait_recv()
+    chosen_mine[...] = chosen_part[people_peer[2]] + chosen_pass[...]
+    send(4, 2, chosen_mine, chosen_far)
+    sends[1, 0].wait_recv()
+    full = jnp.concatenate([gram_sum[0], gram_sum[1]], axis=0)
     lane = lax.broadcasted_iota(jnp.int32, full.shape, 1)
     line = lax.broadcasted_iota(jnp.int32, full.shape, 0)
     full = jnp.where(lane == line + (TILE - k_count), 1.0, full)
@@ -396,11 +424,13 @@
         precision=lax.Precision.HIGHEST,
     )
 
-    for group in (0, 2, 3):
-        for d in (1, 2, 3):
-            sends[group, d].wait_recv()
-    total = next_part[people] + next_in[0] + next_in[1] + next_in[2]
-    chosen = chosen_part[people] + chosen_in[0] + chosen_in[1] + chosen_in[2]
+    for group, d in ((0, 1), (0, 2), (0, 3), (2, 2), (2, 3), (3, 1), (3, 2), (4, 2), (5, 1)):
+        sends[group, d].wait_recv()
+    total = next_part[people] + next_near[...]
+    total = jnp.concatenate(
+        [total[0] + next_in[0] + next_in[1], total[1] + next_far[...]], axis=1
+    )
+    chosen = chosen_part[people] + chosen_near[...] + chosen_far[...]
     scored = resid_score[people] + resid_score_in[0] + resid_score_in[1] + resid_score_in[2]
     solved = exact(inverse, total)
     next_ref[0] = sum3(mm_nt(split3(solved), perm[...]))
@@ -452,7 +482,7 @@
             pltpu.VMEM((n, block, picks), bf16),
             pltpu.VMEM((block, block), bf16),
             pltpu.VMEM((2 * n, block), f32),
-            pltpu.VMEM((n, 2 * k_count, block), bf16),
+            pltpu.VMEM((n, k_count, block), bf16),
             pltpu.VMEM((2, k_count // 2, rows), f32),
             pltpu.VMEM((k_count // 2, rows), f32),
             pltpu.VMEM((k_count // 2, rows), f32),
@@ -460,17 +490,26 @@
             pltpu.VMEM((2, k_count // 2, rows), f32),
             pltpu.VMEM((n, r_count, width), f32),
             pltpu.VMEM((n - 1, r_count, width), f32),
-            pltpu.VMEM((n, k_count, TILE), f32),
-            pltpu.VMEM((n, k_count, block), f32),
-            pltpu.VMEM((n - 1, k_count, block), f32),
+            pltpu.VMEM((2, k_count // 2, TILE), f32),
+            pltpu.VMEM((n, k_count // 2, TILE), f32),
+            pltpu.VMEM((2, k_count // 2, TILE), f32),
+            pltpu.VMEM((n, 2, k_count, block // 2), f32),
+            pltpu.VMEM((2, k_count, block // 2), f32),
+            pltpu.VMEM((2, k_count, block // 2), f32),
+            pltpu.VMEM((k_count, block // 2), f32),
+            pltpu.VMEM((k_count, block // 2), f32),
+            pltpu.VMEM((k_count, block // 2), f32),
             pltpu.VMEM((n, k_count, width), f32),
-            pltpu.VMEM((n - 1, k_count, width), f32),
+            pltpu.VMEM((k_count, width), f32),
+            pltpu.VMEM((k_count, width), f32),
+            pltpu.VMEM((k_count, width), f32),
+            pltpu.VMEM((k_count, width), f32),
             pltpu.SemaphoreType.DMA((len(PIECES),)),
             pltpu.SemaphoreType.DMA((5,)),
             pltpu.SemaphoreType.DMA((3, len(PIECES))),
             pltpu.SemaphoreType.DMA((3, len(PIECES))),
-            pltpu.SemaphoreType.DMA((4, n - 1)),
-            pltpu.SemaphoreType.DMA((4, n - 1)),
+            pltpu.SemaphoreType.DMA((6, n)),
+            pltpu.SemaphoreType.DMA((6, n)),
         ],
         compiler_params=pltpu.CompilerParams(
             collective_id=0, has_side_effects=True, vmem_limit_bytes=62 * 2**20

time: 25.7 us -> 24.3 us (0.946)
  Pallas kernels: 24.9 us -> 23.4 us
    pallas_call x1, Pallas kernels: 24.2 us -> 22.7 us  [fused(): pl.pallas_call(functools.partial(kernel, root_people), out_shape=tuple((p...]
where the time goes in v3:
time: 24.3 us; the launch traced here: 24.1 us
  Pallas kernels  23.4 us (96%)
  between operations  0.64 us (3%)
    pallas_call x1, Pallas kernels, fused(): pl.pallas_call(functools.partial(kernel, root_people), out_shape=tuple((p...  22.7 us
    pallas_call x1, Pallas kernels, fused(): pl.pallas_call(write_results, out_shape=shapes, in_specs=[vmem] * 4, out_...  0.74 us

profile of v3, /device:TPU:0, one launch (start us, length us, event | category | flops | bytes accessed | tf_op | source)
XLA Modules:
  0.0 24.1 jit_solution(16479353491479947700)
XLA Ops:
  0.6 22.7 %shard_map.93 = (f32[32,1536]{1,0:T(8,128)S(1)}, f32[32,64]{1,0:T(8,128)S(1)}, f32[1,32,512]{2,1,0:T(8,128)S(1)}, f32[1,64,128]{2,1,0:T(8,128)S(1)}) custom-call(s32[1536,512]{1,0:T(8,128)} %geno_hbm.1, f32[1,2048]{1,0:T(1,128)} %bitcast.3, f32[12,128]{1,0:T(8,128)} %bitcast.4, bf16[32,2048]{1,0:T(8,128)(2,1)} %basis_hbm.1, bf16[64,1536]{1,0:T(8,128)(2,1)} %resid_hbm.1, ...), custom_call_target="tpu_custom_call" | custom-call | tf_op jit(solution)/shard_map/pallas_call | solution.py:469
  23.3 0.7 %shard_map.94 = (f32[32,1536]{1,0:T(8,128)}, f32[32,64]{1,0:T(8,128)}, f32[1,32,512]{2,1,0:T(8,128)}, f32[1,64,128]{2,1,0:T(8,128)}) custom-call(f32[32,1536]{1,0:T(8,128)S(1)} %get-tuple-element.8.refs_0_, f32[32,64]{1,0:T(8,128)S(1)} %get-tuple-element.9.refs_1_, f32[1,32,512]{2,1,0:T(8,128)S(1)} %get-tuple-element.10.refs_2_, ...), custom_call_target="tpu_custom_call" | custom-call | tf_op jit(solution)/shard_map/pallas_call | solution.py:525

commit v4 on v3

--- a/solution.py
+++ b/solution.py
@@ -83,7 +83,7 @@
 
 
 TILE = 128
-PIECES = (512, 512, 256, 256)
+PIECES = (512, 512, 512)
 
 
 def split2(value):
@@ -234,8 +234,8 @@
         copy = pltpu.make_async_remote_copy(
             src_ref=src,
             dst_ref=dst,
-            send_sem=send_sem.at[group, d],
-            recv_sem=recv_sem.at[group, d],
+            send_sem=send_sem.at[len(sends)],
+            recv_sem=recv_sem.at[len(sends)],
             device_id={"people": people_peer[d]} if d else {"markers": core_peer},
             device_id_type=MESH,
         )
@@ -508,8 +508,8 @@
             pltpu.SemaphoreType.DMA((5,)),
             pltpu.SemaphoreType.DMA((3, len(PIECES))),
             pltpu.SemaphoreType.DMA((3, len(PIECES))),
-            pltpu.SemaphoreType.DMA((6, n)),
-            pltpu.SemaphoreType.DMA((6, n)),
+            pltpu.SemaphoreType.DMA((16,)),
+            pltpu.SemaphoreType.DMA((16,)),
         ],
         compiler_params=pltpu.CompilerParams(
             collective_id=0, has_side_effects=True, vmem_limit_bytes=62 * 2**20

time: 24.3 us -> 23.5 us (0.967)
  Pallas kernels: 23.4 us -> 22.6 us
    pallas_call x1, Pallas kernels: 22.7 us -> 21.9 us  [fused(): pl.pallas_call(functools.partial(kernel, root_people), out_shape=tuple((p...]
where the time goes in v4:
time: 23.5 us; the launch traced here: 23.3 us
  Pallas kernels  22.6 us (96%)
  between operations  0.64 us (3%)
    pallas_call x1, Pallas kernels, fused(): pl.pallas_call(functools.partial(kernel, root_people), out_shape=tuple((p...  21.9 us
    pallas_call x1, Pallas kernels, fused(): pl.pallas_call(write_results, out_shape=shapes, in_specs=[vmem] * 4, out_...  0.74 us

profile of v4, /device:TPU:0, one launch (start us, length us, event | category | flops | bytes accessed | tf_op | source)
XLA Modules:
  0.0 23.3 jit_solution(13183685451109192152)
XLA Ops:
  0.6 21.9 %shard_map.93 = (f32[32,1536]{1,0:T(8,128)S(1)}, f32[32,64]{1,0:T(8,128)S(1)}, f32[1,32,512]{2,1,0:T(8,128)S(1)}, f32[1,64,128]{2,1,0:T(8,128)S(1)}) custom-call(s32[1536,512]{1,0:T(8,128)} %geno_hbm.1, f32[1,2048]{1,0:T(1,128)} %bitcast.3, f32[12,128]{1,0:T(8,128)} %bitcast.4, bf16[32,2048]{1,0:T(8,128)(2,1)} %basis_hbm.1, bf16[64,1536]{1,0:T(8,128)(2,1)} %resid_hbm.1, ...), custom_call_target="tpu_custom_call" | custom-call | tf_op jit(solution)/shard_map/pallas_call | solution.py:469
  22.5 0.7 %shard_map.94 = (f32[32,1536]{1,0:T(8,128)}, f32[32,64]{1,0:T(8,128)}, f32[1,32,512]{2,1,0:T(8,128)}, f32[1,64,128]{2,1,0:T(8,128)}) custom-call(f32[32,1536]{1,0:T(8,128)S(1)} %get-tuple-element.8.refs_0_, f32[32,64]{1,0:T(8,128)S(1)} %get-tuple-element.9.refs_1_, f32[1,32,512]{2,1,0:T(8,128)S(1)} %get-tuple-element.10.refs_2_, ...), custom_call_target="tpu_custom_call" | custom-call | tf_op jit(solution)/shard_map/pallas_call | solution.py:525

commit v5 on v4

--- a/solution.py
+++ b/solution.py
@@ -124,6 +124,22 @@
     return jnp.dot(
         left, right, preferred_element_type=jnp.float32, precision=lax.Precision.HIGHEST
     )
+
+
+def thirds(value):
+    pieces = split3(value)
+    size = value.shape[0]
+    return [pieces[i * size : (i + 1) * size] for i in range(3)]
+
+
+def wide(value):
+    first, second, third = thirds(value)
+    return jnp.concatenate([first, first, second, first, second, third], axis=1)
+
+
+def tall(value):
+    first, second, third = thirds(value)
+    return jnp.concatenate([first, second, first, third, second, first], axis=0)
 
 
 def eliminate(full, count):
@@ -181,6 +197,7 @@
     chosen_mine,
     chosen_pass,
     chosen_far,
+    sketch_tall,
     geno_sem,
     load_sem,
     pair_send,
@@ -365,36 +382,40 @@
         c = people_peer[d]
         freq_row = freq_rows[pl.ds(c, 1), :]
         scale_row = freq_rows[pl.ds(c + n, 1), :]
-        total = (sum2(mm(heavy, dose[c])) - sums * freq_row) * scale_row
-        next_part[c, 0] = total[:, :cut]
-        next_part[c, 1] = total[:, cut:]
-        if d == 3:
-            send(2, 1, next_part.at[c, 1], next_pass)
+        sides = [None, None]
+        for side in (1, 0):
+            at = slice(side * cut, (side + 1) * cut)
+            raw = sum2(mm(heavy, dose[c, :, at]))
+            sides[side] = (raw - sums * freq_row[:, at]) * scale_row[:, at]
+            next_part[c, side] = sides[side]
+            if d == 3 and side:
+                send(2, 1, next_part.at[c, 1], next_pass)
+                pieces = split3(sketch)
+                gram = sum3(mm_nt(pieces, jnp.concatenate([pieces, resid], axis=0)))
+                square = (
+                    gram[:, :k_count]
+                    + gram[:, k_count : 2 * k_count]
+                    + gram[:, 2 * k_count : 3 * k_count]
+                )
+                pad = jnp.zeros((k_count, k_count), jnp.float32)
+                gram = jnp.concatenate([square, gram[:, 3 * k_count :], pad], axis=1)
+                gram_part[0] = gram[:half]
+                gram_part[1] = gram[half:]
+                gram_in[people] = gram_part[core]
+                for far in (3, 2, 1):
+                    send(1, far, gram_part.at[core], gram_in.at[people])
+        total = jnp.concatenate(sides, axis=1)
         if d > 1:
             send(2, d, next_part.at[c, 0], next_in.at[d - 2])
         got = mm(split2(total), hot[c])
         picked = got if picked is None else picked + got
-        if d == 3:
-            pieces = split3(sketch)
-            gram = sum3(mm_nt(pieces, jnp.concatenate([pieces, resid], axis=0)))
-            square = (
-                gram[:, :k_count]
-                + gram[:, k_count : 2 * k_count]
-                + gram[:, 2 * k_count : 3 * k_count]
-            )
-            pad = jnp.zeros((k_count, k_count), jnp.float32)
-            gram = jnp.concatenate([square, gram[:, 3 * k_count :], pad], axis=1)
-            gram_part[0] = gram[:half]
-            gram_part[1] = gram[half:]
-            gram_in[people] = gram_part[core]
-            for far in (3, 2, 1):
-                send(1, far, gram_part.at[core], gram_in.at[people])
     picked = sum2(picked)
     for c in range(n):
         chosen_part[c] = picked[:, c * width : (c + 1) * width]
     send(4, 1, chosen_part.at[people_peer[3]], chosen_pass)
     send(5, 1, chosen_part.at[people_peer[1]], chosen_near)
 
+    sketch_tall[...] = tall(sketch)
     sends[2, 1].wait_recv()
     next_mine[...] = next_part[people_peer[2], 1] + next_pass[...]
     send(3, 2, next_mine, next_far)
@@ -415,7 +436,8 @@
     coef = full[:, k_count : TILE - k_count]
     inverse = full[:, TILE - k_count :]
     coef_ref[...] = coef
-    comp_ref[...] = root_people * exact(inverse, sketch)
+    left = wide(inverse)
+    comp_ref[...] = root_people * mm(left, sketch_tall[...])
     remover = lax.dot_general(
         coef,
         inverse,
@@ -432,8 +454,8 @@
     )
     chosen = chosen_part[people] + chosen_near[...] + chosen_far[...]
     scored = resid_score[people] + resid_score_in[0] + resid_score_in[1] + resid_score_in[2]
-    solved = exact(inverse, total)
-    next_ref[0] = sum3(mm_nt(split3(solved), perm[...]))
+    solved = mm(left, tall(total))
+    next_ref[0] = sum2(mm_nt(split2(solved), perm[...]))
     score_ref[0] = (scored - exact(remover, chosen)) * (1.0 / root_people)
     for copy in list(pairs.values()) + list(sends.values()):
         copy.wait_send()
@@ -504,6 +526,7 @@
             pltpu.VMEM((k_count, width), f32),
             pltpu.VMEM((k_count, width), f32),
             pltpu.VMEM((k_count, width), f32),
+            pltpu.VMEM((6 * k_count, rows), bf16),
             pltpu.SemaphoreType.DMA((len(PIECES),)),
             pltpu.SemaphoreType.DMA((5,)),
             pltpu.SemaphoreType.DMA((3, len(PIECES))),

time: 23.5 us -> 23.1 us (0.983)
  Pallas kernels: 22.6 us -> 22.2 us
    pallas_call x1, Pallas kernels: 21.9 us -> 21.5 us  [fused(): pl.pallas_call(functools.partial(kernel, root_people), out_shape=tuple((p...]
where the time goes in v5:
time: 23.1 us; the launch traced here: 22.9 us
  Pallas kernels  22.2 us (96%)
  between operations  0.64 us (3%)
    pallas_call x1, Pallas kernels, fused(): pl.pallas_call(functools.partial(kernel, root_people), out_shape=tuple((p...  21.5 us
    pallas_call x1, Pallas kernels, fused(): pl.pallas_call(write_results, out_shape=shapes, in_specs=[vmem] * 4, out_...  0.74 us

profile of v5, /device:TPU:0, one launch (start us, length us, event | category | flops | bytes accessed | tf_op | source)
XLA Modules:
  0.0 22.9 jit_solution(13603969177562487415)
XLA Ops:
  0.6 21.5 %shard_map.93 = (f32[32,1536]{1,0:T(8,128)S(1)}, f32[32,64]{1,0:T(8,128)S(1)}, f32[1,32,512]{2,1,0:T(8,128)S(1)}, f32[1,64,128]{2,1,0:T(8,128)S(1)}) custom-call(s32[1536,512]{1,0:T(8,128)} %geno_hbm.1, f32[1,2048]{1,0:T(1,128)} %bitcast.3, f32[12,128]{1,0:T(8,128)} %bitcast.4, bf16[32,2048]{1,0:T(8,128)(2,1)} %basis_hbm.1, bf16[64,1536]{1,0:T(8,128)(2,1)} %resid_hbm.1, ...), custom_call_target="tpu_custom_call" | custom-call | tf_op jit(solution)/shard_map/pallas_call | solution.py:491
  22.1 0.7 %shard_map.94 = (f32[32,1536]{1,0:T(8,128)}, f32[32,64]{1,0:T(8,128)}, f32[1,32,512]{2,1,0:T(8,128)}, f32[1,64,128]{2,1,0:T(8,128)}) custom-call(f32[32,1536]{1,0:T(8,128)S(1)} %get-tuple-element.8.refs_0_, f32[32,64]{1,0:T(8,128)S(1)} %get-tuple-element.9.refs_1_, f32[1,32,512]{2,1,0:T(8,128)S(1)} %get-tuple-element.10.refs_2_, ...), custom_call_target="tpu_custom_call" | custom-call | tf_op jit(solution)/shard_map/pallas_call | solution.py:548

commit v6 on v5

--- a/solution.py
+++ b/solution.py
@@ -305,8 +305,6 @@
         [weight_ref[i : i + 1, :] for i in range(weight_ref.shape[0])], axis=1
     )
 
-    pl.semaphore_wait(barrier, 5)
-
     def forward(i):
         pairs[0, i].wait_recv()
         chip_part[:, spans[i]] = part[core, :, spans[i]] + core_in[:, spans[i]]
@@ -322,14 +320,14 @@
         total = None
         for c in range(n):
             packed = geno[span, c * words : (c + 1) * words]
+            digits = [
+                jnp.bitwise_and(packed, 3),
+                jnp.bitwise_and(jnp.right_shift(packed, 2), 3),
+                jnp.bitwise_and(jnp.right_shift(packed, 4), 3),
+                jnp.right_shift(packed, 6),
+            ]
             tile = jnp.concatenate(
-                [
-                    jnp.bitwise_and(jnp.right_shift(packed, 2 * j), 3)
-                    .astype(jnp.float32)
-                    .astype(jnp.bfloat16)
-                    for j in range(4)
-                ],
-                axis=1,
+                [digit.astype(jnp.float32).astype(jnp.bfloat16) for digit in digits], axis=1
             )
             dose[c, span, :] = tile
             got = mm_nt(basis_rows[c], tile)
@@ -337,6 +335,8 @@
         value = (total - offset) * weight[:, starts[i] : starts[i] + PIECES[i]]
         part[0, :, span] = value[:half]
         part[1, :, span] = value[half:]
+        if i == 0:
+            pl.semaphore_wait(barrier, 5)
         pair(0, i)
         if i:
             forward(i - 1)

time: 23.1 us -> 22.7 us (0.983)
  Pallas kernels: 22.2 us -> 21.9 us
    pallas_call x1, Pallas kernels: 21.5 us -> 21.1 us  [fused(): pl.pallas_call(functools.partial(kernel, root_people), out_shape=tuple((p...]
where the time goes in v6:
time: 22.7 us; the launch traced here: 22.5 us
  Pallas kernels  21.9 us (96%)
  between operations  0.64 us (3%)
    pallas_call x1, Pallas kernels, fused(): pl.pallas_call(functools.partial(kernel, root_people), out_shape=tuple((p...  21.1 us
    pallas_call x1, Pallas kernels, fused(): pl.pallas_call(write_results, out_shape=shapes, in_specs=[vmem] * 4, out_...  0.74 us

profile of v6, /device:TPU:0, one launch (start us, length us, event | category | flops | bytes accessed | tf_op | source)
XLA Modules:
  0.0 22.5 jit_solution(16160897402615425784)
XLA Ops:
  0.6 21.1 %shard_map.93 = (f32[32,1536]{1,0:T(8,128)S(1)}, f32[32,64]{1,0:T(8,128)S(1)}, f32[1,32,512]{2,1,0:T(8,128)S(1)}, f32[1,64,128]{2,1,0:T(8,128)S(1)}) custom-call(s32[1536,512]{1,0:T(8,128)} %geno_hbm.1, f32[1,2048]{1,0:T(1,128)} %bitcast.3, f32[12,128]{1,0:T(8,128)} %bitcast.4, bf16[32,2048]{1,0:T(8,128)(2,1)} %basis_hbm.1, bf16[64,1536]{1,0:T(8,128)(2,1)} %resid_hbm.1, ...), custom_call_target="tpu_custom_call" | custom-call | tf_op jit(solution)/shard_map/pallas_call | solution.py:491
  21.8 0.7 %shard_map.94 = (f32[32,1536]{1,0:T(8,128)}, f32[32,64]{1,0:T(8,128)}, f32[1,32,512]{2,1,0:T(8,128)}, f32[1,64,128]{2,1,0:T(8,128)}) custom-call(f32[32,1536]{1,0:T(8,128)S(1)} %get-tuple-element.8.refs_0_, f32[32,64]{1,0:T(8,128)S(1)} %get-tuple-element.9.refs_1_, f32[1,32,512]{2,1,0:T(8,128)S(1)} %get-tuple-element.10.refs_2_, ...), custom_call_target="tpu_custom_call" | custom-call | tf_op jit(solution)/shard_map/pallas_call | solution.py:548

commit v7 on v6

--- a/solution.py
+++ b/solution.py
@@ -416,6 +416,8 @@
     send(5, 1, chosen_part.at[people_peer[1]], chosen_near)
 
     sketch_tall[...] = tall(sketch)
+    for copy in pairs.values():
+        copy.wait_send()
     sends[2, 1].wait_recv()
     next_mine[...] = next_part[people_peer[2], 1] + next_pass[...]
     send(3, 2, next_mine, next_far)
@@ -457,7 +459,7 @@
     solved = mm(left, tall(total))
     next_ref[0] = sum2(mm_nt(split2(solved), perm[...]))
     score_ref[0] = (scored - exact(remover, chosen)) * (1.0 / root_people)
-    for copy in list(pairs.values()) + list(sends.values()):
+    for copy in sends.values():
         copy.wait_send()
 
 

time: 22.7 us -> 22.7 us (level)
  no operation moved by 1% of the time
where the time goes in v7:
time: 22.7 us; the launch traced here: 22.5 us
  Pallas kernels  21.9 us (96%)
  between operations  0.64 us (3%)
    pallas_call x1, Pallas kernels, fused(): pl.pallas_call(functools.partial(kernel, root_people), out_shape=tuple((p...  21.1 us
    pallas_call x1, Pallas kernels, fused(): pl.pallas_call(write_results, out_shape=shapes, in_specs=[vmem] * 4, out_...  0.74 us

profile of v7, /device:TPU:0, one launch (start us, length us, event | category | flops | bytes accessed | tf_op | source)
XLA Modules:
  0.0 22.5 jit_solution(8303470628992745933)
XLA Ops:
  0.6 21.1 %shard_map.93 = (f32[32,1536]{1,0:T(8,128)S(1)}, f32[32,64]{1,0:T(8,128)S(1)}, f32[1,32,512]{2,1,0:T(8,128)S(1)}, f32[1,64,128]{2,1,0:T(8,128)S(1)}) custom-call(s32[1536,512]{1,0:T(8,128)} %geno_hbm.1, f32[1,2048]{1,0:T(1,128)} %bitcast.3, f32[12,128]{1,0:T(8,128)} %bitcast.4, bf16[32,2048]{1,0:T(8,128)(2,1)} %basis_hbm.1, bf16[64,1536]{1,0:T(8,128)(2,1)} %resid_hbm.1, ...), custom_call_target="tpu_custom_call" | custom-call | tf_op jit(solution)/shard_map/pallas_call | solution.py:493
  21.8 0.7 %shard_map.94 = (f32[32,1536]{1,0:T(8,128)}, f32[32,64]{1,0:T(8,128)}, f32[1,32,512]{2,1,0:T(8,128)}, f32[1,64,128]{2,1,0:T(8,128)}) custom-call(f32[32,1536]{1,0:T(8,128)S(1)} %get-tuple-element.8.refs_0_, f32[32,64]{1,0:T(8,128)S(1)} %get-tuple-element.9.refs_1_, f32[1,32,512]{2,1,0:T(8,128)S(1)} %get-tuple-element.10.refs_2_, ...), custom_call_target="tpu_custom_call" | custom-call | tf_op jit(solution)/shard_map/pallas_call | solution.py:550
